TPU v7x, 32 devices: a whole 2x2x4 slice. The times are simulated.
32 devices in a mesh: grp: 4 (over x, core), rep: 8 (over z, y).
Axes of the slice: x: 2, y: 2, z: 4, core: 2. Of those that a mesh axis runs over, the one named last changes fastest.
Arguments:
- hidden_in: bfloat16 [8, 1024, 1024], P('rep', 'grp'), may hold values from -6 to 6
- doc_ids: int32 [8, 1024], P('rep'), may hold values from 0 to 3, never falling along the last dimension, each value on 1 to 512 neighbouring positions
- ln1_gain: bfloat16 [1024], P('grp'), may hold values from 0.099609375 to 1.8984375
- ln1_bias: bfloat16 [1024], P('grp'), may hold values from -4 to 4
- ln2_gain: bfloat16 [1024], P('grp'), may hold values from 0.099609375 to 1.8984375
- ln2_bias: bfloat16 [1024], P('grp'), may hold values from -4 to 4
- qkv_weight: bfloat16 [1024, 3072], P('grp'), may hold values from -0.1875 to 0.1875
- qkv_bias: bfloat16 [3072], P('grp'), may hold values from -4 to 4
- dense_weight: bfloat16 [1024, 1024], P('grp'), may hold values from -1.5 to 1.5
- dense_bias: bfloat16 [1024], P('grp'), may hold values from -4 to 4
- fc1_weight: bfloat16 [1024, 4096], P('grp'), may hold values from -0.1875 to 0.1875
- fc1_bias: bfloat16 [4096], P('grp'), may hold values from -4 to 4
- fc2_weight: bfloat16 [4096, 1024], P('grp'), may hold values from -0.09375 to 0.09375
- fc2_bias: bfloat16 [1024], P('grp'), may hold values from -4 to 4
- out_grad: bfloat16 [8, 1024, 1024], P('rep', 'grp'), may hold values from -6 to 6
Outputs:
- hidden_out: bfloat16 [8, 1024, 1024], P('rep', 'grp')
- hidden_grad: bfloat16 [8, 1024, 1024], P('rep', 'grp')
- ln1_gain_grad: float32 [1024], P('grp')
- ln1_bias_grad: float32 [1024], P('grp')
- ln2_gain_grad: float32 [1024], P('grp')
- ln2_bias_grad: float32 [1024], P('grp')
- qkv_weight_grad: float32 [1024, 3072], P('grp')
- qkv_bias_grad: float32 [3072], P('grp')
- dense_weight_grad: float32 [1024, 1024], P('grp')
- dense_bias_grad: float32 [1024], P('grp')
- fc1_weight_grad: float32 [1024, 4096], P('grp')
- fc1_bias_grad: float32 [4096], P('grp')
- fc2_weight_grad: float32 [4096, 1024], P('grp')
- fc2_bias_grad: float32 [1024], P('grp')
Inputs may be any that keep to these rules, and one draw needn't show every extreme that they name: `doc_ids`: document numbers never fall along a sequence; each of the 4 documents of a sequence has 1 to 512 tokens, and one has exactly that many.
All inputs are finite; a program needn't handle non-finite values.
Results may differ from a plain program's by a relative error of at most 0.025.
Values may be sent and summed in bfloat16 or wider, within the bound.
A program may use at most 192 MiB of HBM per device.

v0:
```python
import math

import jax
import jax.numpy as jnp
from jax import lax
from jax.sharding import PartitionSpec as P

HEAD_DIM = 64
ROT = 16


EPS = 1e-05
NEG = -1e30


def layer_norm_forward(x, norm_gain_vector, norm_offset_bias):
    row_average = jnp.mean(x, axis=-1, keepdims=True)
    centered_input = x - row_average
    var = jnp.mean(centered_input * centered_input, axis=-1, keepdims=True)
    inverse_deviation = lax.rsqrt(var + EPS)
    normalized_input = centered_input * inverse_deviation
    return (
        normalized_input * norm_gain_vector.astype(jnp.float32)
        + norm_offset_bias.astype(jnp.float32),
        normalized_input,
        inverse_deviation,
    )


def layer_norm_backward(output_gradient, normalized_input, inverse_deviation, norm_gain_vector):
    gain_scaled_grad = output_gradient * norm_gain_vector.astype(jnp.float32)
    projection_term = (
        gain_scaled_grad
        - jnp.mean(gain_scaled_grad, axis=-1, keepdims=True)
        - normalized_input * jnp.mean(gain_scaled_grad * normalized_input, axis=-1, keepdims=True)
    )
    return (
        inverse_deviation * projection_term,
        jnp.sum(output_gradient * normalized_input, axis=0),
        jnp.sum(output_gradient, axis=0),
    )


def rotary_tables(positions, rot):
    half = rot // 2
    freq = 10000.0 ** (-jnp.arange(half, dtype=jnp.float32) / half)
    angle = positions.astype(jnp.float32)[:, None] * freq[None, :]
    return (jnp.cos(angle), jnp.sin(angle))


def rotate(x, cosine, sine, sign):
    half = cosine.shape[1]
    first = x[..., :half]
    second = x[..., half : 2 * half]
    cwide = cosine[:, None, :]
    swide = sign * sine[:, None, :]
    return jnp.concatenate(
        [first * cwide - second * swide, second * cwide + first * swide, x[..., 2 * half :]],
        axis=-1,
    )


def gelu_parts(pre):
    cdf = 0.5 * (1.0 + jax.scipy.special.erf(pre * (1.0 / math.sqrt(2.0))))
    dens = jnp.exp(-0.5 * pre * pre) * (1.0 / math.sqrt(2.0 * math.pi))
    return (pre * cdf, cdf + pre * dens)


def body(
    hidden_in,
    doc_ids,
    ln1_gain,
    ln1_bias,
    ln2_gain,
    ln2_bias,
    qkv_weight,
    qkv_bias,
    dense_weight,
    dense_bias,
    fc1_weight,
    fc1_bias,
    fc2_weight,
    fc2_bias,
    out_grad,
):
    f32 = jnp.float32
    bf16 = jnp.bfloat16
    full = (
        lax.all_gather(ln1_gain, "grp", axis=0, tiled=True),
        lax.all_gather(ln1_bias, "grp", axis=0, tiled=True),
        lax.all_gather(ln2_gain, "grp", axis=0, tiled=True),
        lax.all_gather(ln2_bias, "grp", axis=0, tiled=True),
        lax.all_gather(qkv_weight, "grp", axis=0, tiled=True),
        lax.all_gather(qkv_bias, "grp", axis=0, tiled=True),
        lax.all_gather(dense_weight, "grp", axis=0, tiled=True),
        lax.all_gather(dense_bias, "grp", axis=0, tiled=True),
        lax.all_gather(fc1_weight, "grp", axis=0, tiled=True),
        lax.all_gather(fc1_bias, "grp", axis=0, tiled=True),
        lax.all_gather(fc2_weight, "grp", axis=0, tiled=True),
        lax.all_gather(fc2_bias, "grp", axis=0, tiled=True),
    )
    (
        first_norm_gain,
        first_norm_bias,
        second_norm_gain,
        second_norm_bias,
        wqkv,
        bqkv,
        wd,
        bd,
        w1,
        bf1,
        w2,
        bf2,
    ) = full
    x = hidden_in[0]
    dy = out_grad[0]
    docs = doc_ids[0]
    rows, width = x.shape
    length = docs.shape[0]
    hdim = HEAD_DIM
    heads = width // hdim
    scale = hdim ** (-0.5)
    first = lax.axis_index("grp") * rows
    qpos = first + jnp.arange(rows, dtype=jnp.int32)
    kpos = jnp.arange(length, dtype=jnp.int32)
    qdoc = lax.dynamic_slice_in_dim(docs, first, rows)
    mask = (kpos[None, :] <= qpos[:, None]) & (docs[None, :] == qdoc[:, None])
    cosine, sine = rotary_tables(qpos, ROT)
    input_single_precision = x.astype(f32)
    first_hidden_state, first_normalized_input, first_inverse_deviation = layer_norm_forward(
        input_single_precision, first_norm_gain, first_norm_bias
    )
    second_hidden_state, second_normalized_input, second_inverse_deviation = layer_norm_forward(
        input_single_precision, second_norm_gain, second_norm_bias
    )
    a1 = first_hidden_state.astype(bf16)
    a2 = second_hidden_state.astype(bf16)
    qkv = jnp.dot(a1, wqkv, preferred_element_type=f32) + bqkv.astype(f32)
    query = rotate(qkv[:, :width].reshape(rows, heads, hdim), cosine, sine, 1.0).astype(bf16)
    keyrot = (
        rotate(qkv[:, width : 2 * width].reshape(rows, heads, hdim), cosine, sine, 1.0)
        .astype(bf16)
        .reshape(rows, width)
    )
    value = qkv[:, 2 * width :].astype(bf16)
    all_keys, all_values = (
        lax.all_gather(keyrot, "grp", axis=0, tiled=True),
        lax.all_gather(value, "grp", axis=0, tiled=True),
    )
    all_keys = all_keys.reshape(length, heads, hdim)
    all_values = all_values.reshape(length, heads, hdim)
    scores = jnp.einsum("qhd,khd->hqk", query, all_keys, preferred_element_type=f32) * scale
    scores = jnp.where(mask[None], scores, NEG)
    top = jnp.max(scores, axis=-1, keepdims=True)
    lse = top + jnp.log(jnp.sum(jnp.exp(scores - top), axis=-1, keepdims=True))
    prob = jnp.exp(scores - lse)
    prob_b = prob.astype(bf16)
    mixed = jnp.einsum("hqk,khd->qhd", prob_b, all_values, preferred_element_type=f32).astype(bf16)
    mixed_flat = mixed.reshape(rows, width)
    attn = jnp.dot(mixed_flat, wd, preferred_element_type=f32) + bd.astype(f32)
    pre = jnp.dot(a2, w1, preferred_element_type=f32) + bf1.astype(f32)
    act, slope = gelu_parts(pre)
    gact = act.astype(bf16)
    mlp = jnp.dot(gact, w2, preferred_element_type=f32) + bf2.astype(f32)
    out = (input_single_precision + attn + mlp).astype(bf16)
    (
        first_gain_replica,
        rb1,
        second_gain_replica,
        rb2,
        rwqkv,
        rbqkv,
        rwd,
        rbd,
        rw1,
        rbf1,
        rw2,
        rbf2,
    ) = full
    dyf = dy.astype(f32)
    dbias_out = jnp.sum(dyf, axis=0)
    dpre = jnp.dot(dy, rw2.T, preferred_element_type=f32) * slope
    dbf1 = jnp.sum(dpre, axis=0)
    dpre_b = dpre.astype(bf16)
    second_mlp_input_grad = jnp.dot(dpre_b, rw1.T, preferred_element_type=f32)
    dmix = jnp.dot(dy, rwd.T, preferred_element_type=f32).astype(bf16).reshape(rows, heads, hdim)
    delta = jnp.sum(dmix.astype(f32) * mixed.astype(f32), axis=-1)
    dprob = jnp.einsum("qhd,khd->hqk", dmix, all_values, preferred_element_type=f32)
    dscore = (prob * (dprob - delta.T[:, :, None]) * scale).astype(bf16)
    dquery = jnp.einsum("hqk,khd->qhd", dscore, all_keys, preferred_element_type=f32)
    dkey_full = jnp.einsum("hqk,qhd->khd", dscore, query, preferred_element_type=f32).reshape(
        length, width
    )
    dvalue_full = jnp.einsum("hqk,qhd->khd", prob_b, dmix, preferred_element_type=f32).reshape(
        length, width
    )
    dkey, dvalue = (
        lax.psum_scatter(dkey_full, "grp", scatter_dimension=0, tiled=True),
        lax.psum_scatter(dvalue_full, "grp", scatter_dimension=0, tiled=True),
    )
    dquery = rotate(dquery, cosine, sine, -1.0).reshape(rows, width)
    dkey = rotate(dkey.reshape(rows, heads, hdim), cosine, sine, -1.0).reshape(rows, width)
    dqkv = jnp.concatenate([dquery, dkey, dvalue], axis=1)
    dbqkv = jnp.sum(dqkv, axis=0)
    dqkv_b = dqkv.astype(bf16)
    first_attn_input_grad = jnp.dot(dqkv_b, rwqkv.T, preferred_element_type=f32)
    first_residual_grad, first_norm_gain_grad, first_norm_bias_grad = layer_norm_backward(
        first_attn_input_grad, first_normalized_input, first_inverse_deviation, first_gain_replica
    )
    second_residual_grad, second_norm_gain_grad, second_norm_bias_grad = layer_norm_backward(
        second_mlp_input_grad,
        second_normalized_input,
        second_inverse_deviation,
        second_gain_replica,
    )
    dx = (dyf + first_residual_grad + second_residual_grad).astype(bf16)
    own_a1, own_a2, own_mixed, own_gact = (
        lax.all_to_all(a1, "grp", split_axis=1, concat_axis=0, tiled=True),
        lax.all_to_all(a2, "grp", split_axis=1, concat_axis=0, tiled=True),
        lax.all_to_all(mixed_flat, "grp", split_axis=1, concat_axis=0, tiled=True),
        lax.all_to_all(gact, "grp", split_axis=1, concat_axis=0, tiled=True),
    )
    seq_dqkv, seq_dpre, seq_dy = (
        lax.all_gather(dqkv_b, "grp", axis=0, tiled=True),
        lax.all_gather(dpre_b, "grp", axis=0, tiled=True),
        lax.all_gather(dy, "grp", axis=0, tiled=True),
    )
    s_wqkv = jnp.dot(own_a1.T, seq_dqkv, preferred_element_type=f32)
    s_w1 = jnp.dot(own_a2.T, seq_dpre, preferred_element_type=f32)
    s_wd = jnp.dot(own_mixed.T, seq_dy, preferred_element_type=f32)
    s_w2 = jnp.dot(own_gact.T, seq_dy, preferred_element_type=f32)
    small = (
        lax.psum_scatter(first_norm_gain_grad, "grp", scatter_dimension=0, tiled=True),
        lax.psum_scatter(first_norm_bias_grad, "grp", scatter_dimension=0, tiled=True),
        lax.psum_scatter(second_norm_gain_grad, "grp", scatter_dimension=0, tiled=True),
        lax.psum_scatter(second_norm_bias_grad, "grp", scatter_dimension=0, tiled=True),
        lax.psum_scatter(dbqkv, "grp", scatter_dimension=0, tiled=True),
        lax.psum_scatter(dbias_out, "grp", scatter_dimension=0, tiled=True),
        lax.psum_scatter(dbf1, "grp", scatter_dimension=0, tiled=True),
        lax.psum_scatter(dbias_out, "grp", scatter_dimension=0, tiled=True),
    )
    s_g1, s_b1, s_g2, s_b2, s_bqkv, s_bd, s_bf1, s_bf2 = small
    totals = lax.psum(
        (s_g1, s_b1, s_g2, s_b2, s_wqkv, s_bqkv, s_wd, s_bd, s_w1, s_bf1, s_w2, s_bf2), "rep"
    )
    return (
        out[None],
        dx[None],
        totals[0],
        totals[1],
        totals[2],
        totals[3],
        totals[4],
        totals[5],
        totals[6],
        totals[7],
        totals[8],
        totals[9],
        totals[10],
        totals[11],
    )


def solution(mesh):
    return jax.shard_map(
        body,
        mesh=mesh,
        in_specs=(
            P("rep", "grp", None),
            P("rep", None),
            P("grp"),
            P("grp"),
            P("grp"),
            P("grp"),
            P("grp", None),
            P("grp"),
            P("grp", None),
            P("grp"),
            P("grp", None),
            P("grp"),
            P("grp", None),
            P("grp"),
            P("rep", "grp", None),
        ),
        out_specs=(
            P("rep", "grp", None),
            P("rep", "grp", None),
            P("grp"),
            P("grp"),
            P("grp"),
            P("grp"),
            P("grp", None),
            P("grp"),
            P("grp", None),
            P("grp"),
            P("grp", None),
            P("grp"),
            P("grp", None),
            P("grp"),
        ),
        check_vma=False,
    )
```

profile of v0, /device:TPU:0, one launch (start us, length us, event | category | flops | bytes accessed | tf_op | source)
XLA Modules:
  0.0 930.8 jit_solution(5599721789802756657)
XLA Ops:
  29.8 29.0 %all-gather.18.cloned.1.call-done = bf16[1024,3072]{1,0:T(8,128)(2,1)} async-done(((bf16[256,3072]{1,0:T(8,128)(2,1)}), bf16[1024,3072]{1,0:T(8,128)(2,1)}) %all-gather.18.cloned.1.call-update) | async-done | bytes 6291472 | tf_op jit(solution)/shard_map/all_gather | solution.py:93
  71.7 11.3 %all-gather.24.cloned.1.call-done = bf16[1024,1024]{1,0:T(8,128)(2,1)} async-done(((bf16[256,1024]{1,0:T(8,128)(2,1)}), bf16[1024,1024]{1,0:T(8,128)(2,1)}) %all-gather.24.cloned.1.call-update) | async-done | bytes 2097168 | tf_op jit(solution)/shard_map/all_gather | solution.py:95
  86.3 21.4 %all-gather.20.cloned.1.call-done = bf16[1024,1024]{1,0:T(8,128)(2,1)} async-done(((bf16[256,1024]{1,0:T(8,128)(2,1)}), bf16[1024,1024]{1,0:T(8,128)(2,1)}) %all-gather.20.cloned.1.call-update) | async-done | bytes 2097168 | tf_op jit(solution)/shard_map/all_gather | solution.py:149
  110.6 22.0 %all-gather.22.cloned.1.call-done = bf16[1024,1024]{0,1:T(8,128)(2,1)} async-done(((bf16[256,1024]{0,1:T(8,128)(2,1)}), bf16[1024,1024]{0,1:T(8,128)(2,1)}) %all-gather.22.cloned.1.call-update) | async-done | bytes 2097168 | tf_op jit(solution)/shard_map/all_gather | solution.py:148
  150.0 9.9 %multiply_convert_fusion = bf16[16,256,1024]{2,1,0:T(8,128)(2,1)S(1)} fusion(f32[16,256,1024]{2,1,0:T(8,128)} %copy-done, bf16[256,16,64]{0,2,1:T(8,128)(2,1)S(1)} %bitcast.159, bf16[1024,16,64]{0,2,1:T(8,128)(2,1)S(1)} %bitcast.155, f32[16,256]{1,0:T(8,128)S(1)} %bitcast.182, f32[16,256]{1,0:T(8,128)S(1)} %log_add_fusion, pred[256,1024]{1,0:T(8,128)(4,1)S(1)} %fusion.19), kind=kOutput, calls=%fused_computation | convolution fusion | flops 566231040 | bytes 28082176 | tf_op jit(solution)/shard_map/qhd,khd->hqk/dot_general | solution.py:189
  165.5 10.3 %fusion.34 = f32[16,64,1024]{2,1,0:T(8,128)} fusion(bf16[256,16,64]{0,2,1:T(8,128)(2,1)S(1)} %bitcast.160, f32[16,256,1024]{2,1,0:T(8,128)} %copy-done, f32[16,256]{1,0:T(8,128)S(1)} %log_add_fusion, pred[256,1024]{1,0:T(8,128)(4,1)S(1)} %fusion.19), kind=kOutput, calls=%fused_computation.84 | convolution fusion | flops 553648128 | bytes 21774336 | tf_op jit(solution)/shard_map/hqk,qhd->khd/dot_general | solution.py:195
  192.4 8.6 multiply_convert_fusion.1
  201.0 51.1 %all-gather.28.cloned.1.call-done = bf16[4096,1024]{1,0:T(8,128)(2,1)} async-done(((bf16[1024,1024]{1,0:T(8,128)(2,1)}), bf16[4096,1024]{1,0:T(8,128)(2,1)}) %all-gather.28.cloned.1.call-update) | async-done | bytes 8388624 | tf_op jit(solution)/shard_map/all_gather | solution.py:99
  252.1 7.6 fusion.44
  259.8 6.9 convolution_bitcast_fusion
  267.8 31.4 %reduce-scatter.3.cloned.1.call-done = f32[256,1024]{0,1:T(8,128)} async-done(((f32[1024,1024]{0,1:T(8,128)}), f32[256,1024]{0,1:T(8,128)}) %reduce-scatter.3.cloned.1.call-update) | async-done | bytes 1048592 | tf_op jit(solution)/shard_map/reduce_scatter | solution.py:199
  301.7 45.3 %reduce-scatter.5.cloned.1.call-done = f32[256,1024]{0,1:T(8,128)} async-done(((f32[1024,1024]{0,1:T(8,128)}), f32[256,1024]{0,1:T(8,128)}) %reduce-scatter.5.cloned.1.call-update) | async-done | bytes 1048592 | tf_op jit(solution)/shard_map/reduce_scatter | solution.py:200
  357.3 10.6 %all-to-all-done.1 = bf16[256,4,256]{2,0,1:T(8,128)(2,1)S(1)} async-done(((bf16[256,4,256]{2,0,1:T(8,128)(2,1)}), bf16[256,4,256]{2,0,1:T(8,128)(2,1)S(1)}, u32[]{:S(2)}, u32[]{:S(2)}) %all-to-all-start.1) | async-done | bytes 524320 | tf_op jit(solution)/shard_map/all_to_all | solution.py:221
  379.7 28.1 %all-to-all-done.3 = bf16[256,4,1024]{2,0,1:T(8,128)(2,1)} async-done(((bf16[256,4,1024]{2,0,1:T(8,128)(2,1)}), bf16[256,4,1024]{2,0,1:T(8,128)(2,1)}, u32[]{:S(2)}, u32[]{:S(2)}) %all-to-all-start.3) | async-done | bytes 2097184 | tf_op jit(solution)/shard_map/all_to_all | solution.py:222
  411.3 6.6 fusion.8
  417.9 8.1 all-to-all-done.2
  430.4 25.5 %all-gather.32.cloned.1.call-done = bf16[1024,4096]{1,0:T(8,128)(2,1)} async-done(((bf16[256,4096]{1,0:T(8,128)(2,1)}), bf16[1024,4096]{1,0:T(8,128)(2,1)}) %all-gather.32.cloned.1.call-update) | async-done | bytes 8388624 | tf_op jit(solution)/shard_map/all_gather | solution.py:226
  455.9 7.8 fusion.48
  463.7 41.0 %all-gather.30.cloned.1.call-done = bf16[1024,3072]{0,1:T(8,128)(2,1)} async-done(((bf16[256,3072]{0,1:T(8,128)(2,1)}), bf16[1024,3072]{0,1:T(8,128)(2,1)}) %all-gather.30.cloned.1.call-update) | async-done | bytes 6291472 | tf_op jit(solution)/shard_map/all_gather | solution.py:225
  504.8 6.5 fusion.47
  524.6 6.6 convolution_add_fusion.3
  539.9 11.6 %all-reduce.9 = (f32[1024]{0:T(1024)S(1)}, f32[1024]{0:T(1024)S(1)}, f32[1024]{0:T(1024)S(1)}, f32[1024]{0:T(1024)S(1)}, f32[3072]{0:T(1024)S(1)}, /*index=5*/f32[1024]{0:T(1024)S(1)}, f32[4096]{0:T(1024)S(1)}) all-reduce(f32[1024]{0:T(1024)S(1)} %get-tuple-element.16, ...), channel_id=5, replica_groups=mesh['grp'=4,'rep'=8] {'grp'}, use_global_device_ids=true, to_apply=%region_12.13.clone | all-reduce | flops 12288 | bytes 98304
  551.9 40.0 %all-reduce.7 = (f32[256]{0:T(256)}, f32[256]{0:T(256)}, f32[256]{0:T(256)}, f32[256]{0:T(256)}, f32[768]{0:T(1024)}, /*index=5*/f32[256]{0:T(256)S(1)}, f32[1024]{0:T(1024)}) all-reduce(f32[256]{0:T(256)S(1)} %dynamic-slice.2, f32[256]{0:T(256)S(1)} %dynamic-slice.4, ...), channel_id=1, replica_groups=mesh['grp'=4,'rep'=8] {'rep'}, use_global_device_ids=true, to_apply=%region_13.14 | all-reduce | flops 3072 | bytes 24576 | tf_op jit(solution)/shard_map/psum | solution.py:244
  591.9 320.6 %all-reduce.12.cloned.1.call-done = (f32[256,3072]{1,0:T(8,128)}, f32[256,1024]{1,0:T(8,128)}, f32[256,4096]{1,0:T(8,128)}, f32[1024,1024]{1,0:T(8,128)}) async-done(((f32[256,3072]{1,0:T(8,128)}, f32[256,1024]{1,0:T(8,128)}, f32[256,4096]{1,0:T(8,128)}, f32[1024,1024]{1,0:T(8,128)}), (f32[256,3072]{1,0:T(8,128)}, f32[256,1024]{1,0:T(8,128)}, f32[256,4096]{1,0:T(8,128)}, ...) | async-done | bytes 12582928 | tf_op jit(solution)/shard_map/psum | solution.py:244
  (183 shorter events, 146.2 us)
Async XLA Ops:
  7.2 51.6 %all-gather.18.cloned.1.call-start = ((), (), s32[]{:S(2)}) async-start(), calls=%async_computation.6 | async-start | bytes 7864320 | tf_op jit(solution)/shard_map/all_gather | solution.py:93
  7.9 75.0 %all-gather.24.cloned.1.call-start = ((), (), s32[]{:S(2)}) async-start(), calls=%async_computation.9 | async-start | bytes 2621440 | tf_op jit(solution)/shard_map/all_gather | solution.py:95
  8.7 99.1 %all-gather.20.cloned.1.call-start = ((), (), s32[]{:S(2)}) async-start(), calls=%async_computation.7 | async-start | bytes 2621440 | tf_op jit(solution)/shard_map/all_gather | solution.py:149
  66.2 66.4 %all-gather.22.cloned.1.call-start = ((), (), s32[]{:S(2)}) async-start(), calls=%async_computation.8 | async-start | bytes 2621440 | tf_op jit(solution)/shard_map/all_gather | solution.py:148
  69.1 13.9 %copy-start.10 = (bf16[1,256,1024]{2,1,0:T(8,128)(2,1)S(1)}, bf16[1,256,1024]{2,1,0:T(8,128)(2,1)}, u32[]{:S(2)}) copy-start(bf16[1,256,1024]{2,1,0:T(8,128)(2,1)} %param.29) | copy-start | bytes 1572868
  69.9 122.4 %all-gather.26.cloned.1.call-start = ((), (), s32[]{:S(2)}) async-start(), calls=%async_computation.10 | async-start | bytes 10485760 | tf_op jit(solution)/shard_map/all_gather | solution.py:97
  70.5 181.6 %all-gather.28.cloned.1.call-start = ((), (), s32[]{:S(2)}) async-start(), calls=%async_computation.11 | async-start | bytes 10485760 | tf_op jit(solution)/shard_map/all_gather | solution.py:99
  71.1 228.1 %reduce-scatter.3.cloned.1.call-start = ((), (), s32[]{:S(2)}) async-start(), calls=%async_computation.12 | async-start | bytes 5242880 | tf_op jit(solution)/shard_map/reduce_scatter | solution.py:199
  164.5 182.5 %reduce-scatter.5.cloned.1.call-start = ((), (), s32[]{:S(2)}) async-start(), calls=%async_computation.13 | async-start | bytes 5242880 | tf_op jit(solution)/shard_map/reduce_scatter | solution.py:200
  175.8 11.0 %copy-start.21 = (bf16[1024]{0:T(1024)(128)(2,1)S(1)}, bf16[1024]{0:T(1024)(128)(2,1)}, u32[]{:S(2)}) copy-start(bf16[1024]{0:T(1024)(128)(2,1)} %param.26) | copy-start | bytes 6148
  175.8 16.6 %copy-start.2 = (bf16[1,256,1024]{2,1,0:T(8,128)(2,1)S(1)}, bf16[1,256,1024]{2,1,0:T(8,128)(2,1)}, u32[]{:S(2)}) copy-start(bf16[1,256,1024]{2,1,0:T(8,128)(2,1)} %param.15) | copy-start | bytes 1572868
  175.8 200.6 %all-gather.34.cloned.1.call-start = ((), (), s32[]{:S(2)}) async-start(), calls=%async_computation.16 | async-start | bytes 2621440 | tf_op jit(solution)/shard_map/all_gather | solution.py:227
  176.6 279.4 %all-gather.32.cloned.1.call-start = ((), (), s32[]{:S(2)}) async-start(), calls=%async_computation.15 | async-start | bytes 10485760 | tf_op jit(solution)/shard_map/all_gather | solution.py:226
  192.4 59.8 %copy-start.11 = (bf16[1,256,1024]{2,1,0:T(8,128)(2,1)S(1)}, bf16[1,256,1024]{2,1,0:T(8,128)(2,1)}, u32[]{:S(2)}) copy-start(bf16[1,256,1024]{2,1,0:T(8,128)(2,1)} %param.29) | copy-start | bytes 1572868
  259.8 245.0 %all-gather.30.cloned.1.call-start = ((), (), s32[]{:S(2)}) async-start(), calls=%async_computation.14 | async-start | bytes 7864320 | tf_op jit(solution)/shard_map/all_gather | solution.py:225
  301.7 47.8 %copy-start.13 = (bf16[16,64,256]{2,1,0:T(8,128)(2,1)S(1)}, bf16[16,64,256]{2,1,0:T(8,128)(2,1)}, u32[]{:S(2)}) copy-start(bf16[16,64,256]{2,1,0:T(8,128)(2,1)} %get-tuple-element.72) | copy-start | bytes 1572868
  350.5 17.3 %all-to-all-start.1 = ((bf16[256,4,256]{2,0,1:T(8,128)(2,1)}), bf16[256,4,256]{2,0,1:T(8,128)(2,1)S(1)}, u32[]{:S(2)}, u32[]{:S(2)}) async-start(bf16[256,4,256]{2,0,1:T(8,128)(2,1)} %copy.52), calls=%async_computation.3 | async-start | bytes 1048576 | tf_op jit(solution)/shard_map/all_to_all | solution.py:221
  367.9 39.9 %all-to-all-start.3 = ((bf16[256,4,1024]{2,0,1:T(8,128)(2,1)}), bf16[256,4,1024]{2,0,1:T(8,128)(2,1)}, u32[]{:S(2)}, u32[]{:S(2)}) async-start(bf16[256,4,1024]{2,0,1:T(8,128)(2,1)} %bitcast.141), calls=%async_computation.5 | async-start | bytes 4194304 | tf_op jit(solution)/shard_map/all_to_all | solution.py:222
  407.8 18.3 %all-to-all-start.2 = ((bf16[256,4,256]{2,0,1:T(8,128)(2,1)}), bf16[256,4,256]{2,0,1:T(8,128)(2,1)S(1)}, u32[]{:S(2)}, u32[]{:S(2)}) async-start(bf16[256,4,256]{2,0,1:T(8,128)(2,1)} %get-tuple-element.56), calls=%async_computation.4 | async-start | bytes 1048576 | tf_op jit(solution)/shard_map/all_to_all | solution.py:220
  426.0 37.7 %all-to-all-start = ((bf16[256,4,256]{2,0,1:T(8,128)(2,1)}), bf16[256,4,256]{2,0,1:T(8,128)(2,1)}, u32[]{:S(2)}, u32[]{:S(2)}) async-start(bf16[256,4,256]{2,0,1:T(8,128)(2,1)} %get-tuple-element.57), calls=%async_computation.2 | async-start | bytes 1048576 | tf_op jit(solution)/shard_map/all_to_all | solution.py:219
  430.2 482.3 %all-reduce.12.cloned.1.call-start = ((), (), s32[]{:S(2)}) async-start(), calls=%async_computation.17 | async-start | bytes 25165824 | tf_op jit(solution)/shard_map/psum | solution.py:244
  524.6 8.2 slice-start
  524.6 8.2 slice-start.1
  591.9 326.2 %copy-start.22 = (f32[256]{0:T(256)}, f32[256]{0:T(256)S(1)}, u32[]{:S(2)}) copy-start(f32[256]{0:T(256)S(1)} %get-tuple-element.114) | copy-start | bytes 3076
  (24 other events, 85.9 us)
Sparse Core Ops, SparseCore 0:
  9.6 49.1 all-gather.17
  60.3 22.5 all-gather.23
  85.1 22.6 all-gather.19
  109.7 22.8 all-gather.21
  134.0 58.3 all-gather.25
  193.8 58.3 all-gather.27
  254.6 44.4 reduce-scatter.2
  302.4 44.4 reduce-scatter.4
  348.5 27.0 all-gather.33
  377.0 78.8 all-gather.31
  457.5 47.2 all-gather.29
  511.4 401.0 all-reduce.11
where the time goes:
time: 935 us; the launch traced here: 931 us
  waiting for transfers between devices  649 us (69%)
  matrix products  101 us (11%)
  blocking collectives  93.8 us (10%)
  local copies, waits for them, and re-layouts  36.8 us (4%)
  between operations  17 us (2%)
  other arithmetic  16.8 us (2%)
  starting transfers between devices  16.4 us (2%)
    psum x1, waiting for transfers between devices, body(): lax.psum((s_g1, s_b1, s_g2, s_b2, s_wqkv, s_bqkv, s_wd, s_bd, s_w1, s_bf1...  321 us
    all_gather x1, waiting for transfers between devices, body(): lax.all_gather(fc2_weight, 'grp', axis=0, tiled=True)  51.1 us
    reduce_scatter x1, waiting for transfers between devices, body(): lax.psum_scatter(dvalue_full, 'grp', scatter_dimension=0, tiled=True)  45.3 us
    all_gather x1, waiting for transfers between devices, body(): lax.all_gather(dqkv_b, 'grp', axis=0, tiled=True)  41 us
    psum x1, blocking collectives, body(): lax.psum((s_g1, s_b1, s_g2, s_b2, s_wqkv, s_bqkv, s_wd, s_bd, s_w1, s_bf1...  40 us
    reduce_scatter x1, waiting for transfers between devices, body(): lax.psum_scatter(dkey_full, 'grp', scatter_dimension=0, tiled=True)  31.4 us
    all_gather x1, waiting for transfers between devices, body(): lax.all_gather(qkv_weight, 'grp', axis=0, tiled=True)  29 us
    all_to_all x1, waiting for transfers between devices, body(): lax.all_to_all(gact, 'grp', split_axis=1, concat_axis=0, tiled=True)  28.1 us
  transfers between devices with their start and end apart: 16, of which 13 were waited for; matrix products, arithmetic and copies ran while one was open for 14% of the time, Pallas kernels for 0%

commit v1 on v0

v1 whole, which is shorter than its diff:
```python
import functools
import math

import jax
import jax.numpy as jnp
import numpy as np
from jax import lax
from jax.experimental import pallas as pl
from jax.experimental.pallas import tpu as pltpu
from jax.sharding import PartitionSpec as P

HEAD_DIM = 64
ROT = 16
EPS = 1e-05
NEG = -1e30
DOC_MAX = 512
PAIR = 128

f32 = jnp.float32
bf16 = jnp.bfloat16


def rotary_tables(length):
    half = ROT // 2
    freq = 10000.0 ** (-np.arange(half, dtype=np.float64) / half)
    angle = np.arange(length, dtype=np.float64)[:, None] * freq[None, :]
    cos = np.ones((length, HEAD_DIM))
    low = np.zeros((length, HEAD_DIM))
    high = np.zeros((length, HEAD_DIM))
    cos[:, :half] = np.cos(angle)
    cos[:, half : 2 * half] = np.cos(angle)
    low[:, :half] = -np.sin(angle)
    high[:, half : 2 * half] = np.sin(angle)
    reps = PAIR // HEAD_DIM
    return tuple(np.tile(t, (1, reps)).astype(np.float32) for t in (cos, low, high))


def rotate(x, cos, low, high, sign):
    half = ROT // 2
    up = pltpu.roll(x, PAIR - half, 1)
    down = pltpu.roll(x, half, 1)
    return x * cos + sign * (up * low + down * high)


def dot_nt(a, b):
    return lax.dot_general(a, b, (((1,), (1,)), ((), ())), preferred_element_type=f32)


def dot_tn(a, b):
    return lax.dot_general(a, b, (((0,), (0,)), ((), ())), preferred_element_type=f32)


def attention_kernel(
    block,
    q_ref,
    k_ref,
    v_ref,
    dmix_ref,
    drow_ref,
    dcol_ref,
    cos_ref,
    low_ref,
    high_ref,
    mix_ref,
    dq_ref,
    dk_ref,
    dv_ref,
    bias_ref,
    qs,
    ks,
    vs,
    dks,
    dvs,
):
    length = q_ref.shape[0]
    scale = HEAD_DIM ** (-0.5)
    tables = (cos_ref[...], low_ref[...], high_ref[...])
    qs[...] = rotate(q_ref[...], *tables, 1.0).astype(bf16)
    ks[...] = rotate(k_ref[...], *tables, 1.0).astype(bf16)
    vs[...] = v_ref[...].astype(bf16)
    dks[...] = jnp.zeros_like(dks)
    dvs[...] = jnp.zeros_like(dvs)
    dq_sum = jnp.zeros((1, PAIR), f32)
    reach = -(-(DOC_MAX - 1) // block)
    for i in range(length // block):
        first = max(0, i - reach) * block
        end = (i + 1) * block
        wide = end - first
        rows = pl.ds(i * block, block)
        keys = pl.ds(first, wide)
        q = qs[rows, :]
        dmix = dmix_ref[rows, :]
        k = ks[keys, :]
        v = vs[keys, :]
        qpos = i * block + lax.broadcasted_iota(jnp.int32, (block, wide), 0)
        kpos = first + lax.broadcasted_iota(jnp.int32, (block, wide), 1)
        allowed = (kpos <= qpos) & (dcol_ref[rows, :] == drow_ref[:, first:end])
        lane = lax.broadcasted_iota(jnp.int32, (block, PAIR), 1)
        wide_lane = lax.broadcasted_iota(jnp.int32, (wide, PAIR), 1)
        mix = dq = None
        for h in range(PAIR // HEAD_DIM):
            mine = (lane // HEAD_DIM) == h
            zero = jnp.zeros((block, PAIR), bf16)
            qh = jnp.where(mine, q, zero)
            dmixh = jnp.where(mine, dmix, zero)
            s = jnp.where(allowed, dot_nt(qh, k) * scale, NEG)
            top = jnp.max(s, axis=1, keepdims=True)
            e = jnp.exp(s - top)
            p = e * (1.0 / jnp.sum(e, axis=1, keepdims=True))
            pb = p.astype(bf16)
            o = jnp.dot(pb, v, preferred_element_type=f32).astype(bf16)
            o = jnp.where(mine, o, zero)
            delta = jnp.sum(o.astype(f32) * dmixh.astype(f32), axis=1, keepdims=True)
            dp = dot_nt(dmixh, v)
            ds = (p * (dp - delta) * scale).astype(bf16)
            dqh = jnp.dot(ds, k, preferred_element_type=f32)
            mix = o if h == 0 else mix + o
            dq = jnp.where(mine, dqh, 0.0) if h == 0 else jnp.where(mine, dqh, dq)
            dks[keys, :] += dot_tn(ds, qh)
            dvs[keys, :] += dot_tn(pb, dmixh)
        mix_ref[rows, :] = mix
        dq = rotate(dq, cos_ref[rows, :], low_ref[rows, :], high_ref[rows, :], -1.0)
        dq_sum = dq_sum + jnp.sum(dq, axis=0, keepdims=True)
        dq_ref[rows, :] = dq.astype(bf16)
    dk = rotate(dks[...], *tables, -1.0)
    dv = dvs[...]
    dk_ref[...] = dk.astype(bf16)
    dv_ref[...] = dv.astype(bf16)
    bias_ref[0:1, :] = dq_sum
    bias_ref[1:2, :] = jnp.sum(dk, axis=0, keepdims=True)
    bias_ref[2:3, :] = jnp.sum(dv, axis=0, keepdims=True)
    bias_ref[3:8, :] = jnp.zeros((5, PAIR), f32)


def attention(qkv, dmix, docs):
    length, width = dmix.shape
    pairs = width // PAIR
    block = 256
    col = lambda off: pl.BlockSpec((length, PAIR), lambda h: (0, off + h))
    whole = lambda shape: pl.BlockSpec(shape, lambda h: (0, 0))
    tables = [jnp.asarray(t) for t in rotary_tables(length)]
    out = lambda: jax.ShapeDtypeStruct((length, width), bf16)
    return pl.pallas_call(
        functools.partial(attention_kernel, block),
        grid=(pairs,),
        in_specs=[col(0), col(pairs), col(2 * pairs), col(0)]
        + [whole((1, length)), whole((length, 1))]
        + [whole((length, PAIR))] * 3,
        out_specs=[col(0)] * 4 + [pl.BlockSpec((8, PAIR), lambda h: (0, h))],
        out_shape=[out(), out(), out(), out(), jax.ShapeDtypeStruct((8, width), f32)],
        scratch_shapes=[pltpu.VMEM((length, PAIR), bf16)] * 3
        + [pltpu.VMEM((length, PAIR), f32)] * 2,
        compiler_params=pltpu.CompilerParams(vmem_limit_bytes=40 * 1024 * 1024),
        cost_estimate=pl.CostEstimate(
            flops=10 * length * length * width, bytes_accessed=length * width * 24, transcendentals=length * length * 4
        ),
    )(qkv, qkv, qkv, dmix, docs[None, :], docs[:, None], *tables)


def gelu_parts(pre):
    cdf = 0.5 * (1.0 + lax.erf(pre * (1.0 / math.sqrt(2.0))))
    dens = jnp.exp(-0.5 * pre * pre) * (1.0 / math.sqrt(2.0 * math.pi))
    return (pre * cdf, cdf + pre * dens)


def body(
    groups,
    reps,
    hidden_in,
    doc_ids,
    ln1_gain,
    ln1_bias,
    ln2_gain,
    ln2_bias,
    qkv_weight,
    qkv_bias,
    dense_weight,
    dense_bias,
    fc1_weight,
    fc1_bias,
    fc2_weight,
    fc2_bias,
    out_grad,
):
    own = lax.axis_index("grp")
    x_own = hidden_in[0]
    dy_own = out_grad[0]
    docs = doc_ids[0]
    rows, width = x_own.shape
    length = docs.shape[0]
    part = width // groups
    hidden = fc1_weight.shape[1] // groups

    x = lax.all_gather(x_own, "grp", axis=0, tiled=True)
    dy = lax.all_gather(dy_own, "grp", axis=0, tiled=True)
    vectors = (ln1_gain, ln1_bias, ln2_gain, ln2_bias, qkv_bias, dense_bias, fc2_bias)
    packed = lax.all_gather(jnp.concatenate(vectors), "grp", axis=0, tiled=False)
    cuts = np.cumsum([v.shape[0] for v in vectors])[:-1].tolist()
    gain1, bias1, gain2, bias2, bqkv, bd, b2 = (
        t.reshape(-1).astype(f32) for t in jnp.split(packed, cuts, axis=1)
    )
    bqkv = lax.dynamic_slice_in_dim(bqkv.reshape(3, groups, part), own, 1, 1).reshape(-1)
    wqkv = lax.all_to_all(
        qkv_weight.reshape(part, 3, groups, part), "grp", split_axis=2, concat_axis=0, tiled=True
    ).reshape(width, 3 * part)
    w1 = lax.all_to_all(fc1_weight, "grp", split_axis=1, concat_axis=0, tiled=True)
    wd = dense_weight
    w2 = fc2_weight

    def reduce_rows(grad):
        piece = lax.psum_scatter(grad.astype(bf16), "rep", scatter_dimension=0, tiled=True)
        return lax.all_gather(piece, "rep", axis=0, tiled=True).astype(f32)

    def reduce_columns(grad, blocks):
        cols = grad.shape[1]
        g = grad.astype(bf16).reshape(groups, reps, part // reps, cols)
        g = g.transpose(1, 0, 2, 3).reshape(width, cols)
        piece = lax.psum_scatter(g, "rep", scatter_dimension=0, tiled=True)
        piece = piece.reshape(groups, part // reps, cols)
        piece = lax.all_to_all(piece, "grp", split_axis=0, concat_axis=0, tiled=True)
        piece = piece.reshape(groups, part // reps, blocks, cols // blocks)
        piece = piece.transpose(1, 2, 0, 3).reshape(part // reps, groups * cols)
        return lax.all_gather(piece, "rep", axis=0, tiled=True).astype(f32)

    def normalize(t):
        t = t.astype(f32)
        centered = t - jnp.mean(t, axis=-1, keepdims=True)
        var = jnp.mean(centered * centered, axis=-1, keepdims=True)
        rstd = lax.rsqrt(var + EPS)
        return centered * rstd, rstd

    xhat, _ = normalize(x)
    a1 = (xhat * gain1 + bias1).astype(bf16)
    a2 = (xhat * gain2 + bias2).astype(bf16)

    dmix = dot_nt(dy, wd).astype(bf16)
    qkv = jnp.dot(a1, wqkv, preferred_element_type=f32) + bqkv
    mixed, dq, dk, dv, dbqkv = attention(qkv, dmix, docs)

    pre = jnp.dot(a2, w1, preferred_element_type=f32) + fc1_bias.astype(f32)
    act, slope = gelu_parts(pre)
    gact = act.astype(bf16)
    g_w2 = reduce_rows(dot_tn(gact, dy))
    dpre = dot_nt(dy, w2) * slope
    dbf1 = jnp.sum(dpre, axis=0)
    dpre_b = dpre.astype(bf16)
    g_w1 = reduce_columns(dot_tn(a2, dpre_b), 1)
    da2 = dot_nt(dpre_b, w1)

    g_wd = reduce_rows(dot_tn(mixed, dy))
    dqkv = jnp.concatenate([dq, dk, dv], axis=1)
    g_wqkv = reduce_columns(dot_tn(a1, dqkv), 3)
    da1 = dot_nt(dqkv, wqkv)

    branch = jnp.dot(mixed, wd, preferred_element_type=f32) + jnp.dot(
        gact, w2, preferred_element_type=f32
    )
    branch = lax.psum_scatter(branch.astype(bf16), "grp", scatter_dimension=0, tiled=True)
    out = (x_own.astype(f32) + branch.astype(f32) + (bd + b2)).astype(bf16)

    grad = (da1 * gain1 + da2 * gain2).astype(bf16)
    grad = lax.psum_scatter(grad, "grp", scatter_dimension=0, tiled=True).astype(f32)
    xhat_own, rstd_own = normalize(x_own)
    inner = (
        grad
        - jnp.mean(grad, axis=-1, keepdims=True)
        - xhat_own * jnp.mean(grad * xhat_own, axis=-1, keepdims=True)
    )
    dx = (dy_own.astype(f32) + rstd_own * inner).astype(bf16)

    wide = lambda v, n: lax.dynamic_update_slice_in_dim(jnp.zeros((n * v.shape[0],), f32), v, own * v.shape[0], 0)
    bq = lax.dynamic_update_slice(
        jnp.zeros((3, groups, part), f32), dbqkv[:3].reshape(3, 1, part), (0, own, 0)
    ).reshape(-1)
    pieces = (
        jnp.sum(da1 * xhat, axis=0),
        jnp.sum(da1, axis=0),
        jnp.sum(da2 * xhat, axis=0),
        jnp.sum(da2, axis=0),
        jnp.sum(dy_own.astype(f32), axis=0),
        bq,
        wide(dbf1, groups),
    )
    flat = jnp.concatenate([p.reshape(groups, -1) for p in pieces], axis=1)
    flat = lax.psum(flat, ("grp", "rep"))
    flat = lax.dynamic_slice_in_dim(flat, own, 1, 0)[0]
    cuts = np.cumsum([p.shape[0] // groups for p in pieces])[:-1].tolist()
    s_g1, s_b1, s_g2, s_b2, s_bd, s_bqkv, s_bf1 = jnp.split(flat, cuts)
    return (
        out[None],
        dx[None],
        s_g1,
        s_b1,
        s_g2,
        s_b2,
        g_wqkv,
        s_bqkv,
        g_wd,
        s_bd,
        g_w1,
        s_bf1,
        g_w2,
        s_bd,
    )


def solution(mesh):
    vec = P("grp")
    mat = P("grp", None)
    tok = P("rep", "grp", None)
    return jax.shard_map(
        functools.partial(body, mesh.shape["grp"], mesh.shape["rep"]),
        mesh=mesh,
        in_specs=(tok, P("rep", None), vec, vec, vec, vec, mat, vec, mat, vec, mat, vec, mat, vec, tok),
        out_specs=(tok, tok, vec, vec, vec, vec, mat, vec, mat, vec, mat, vec, mat, vec),
        check_vma=False,
    )
```

time: 935 us -> 601 us (0.64)
  waiting for transfers between devices: 649 us -> 335 us
  matrix products: 101 us -> 44.6 us
  blocking collectives: 93.8 us -> 121 us
  Pallas kernels: 0 us -> 17.7 us
    psum x1 -> x0, waiting for transfers between devices: 321 us -> none  [body(): lax.psum((s_g1, s_b1, s_g2, s_b2, s_wqkv, s_bqkv, s_wd, s_bd, s_w1, s_bf1...]
    reduce_scatter x2 -> x6, waiting for transfers between devices: 76.6 us -> 160 us  [the longest x2 70.6 us: reduce_columns(): piece = lax.psum_scatter(g, 'rep', scatter_dimension=0, tiled=True)]
    dot_general x18 -> x12, matrix products: 101 us -> 44.6 us  [the longest x4 17.7 us: dot_nt(): lax.dot_general(a, b, (((1,), (1,)), ((), ())), preferred_element_type=f32)]
    all_gather x9 -> x5, waiting for transfers between devices: 201 us -> 148 us  [the longest x2 90.2 us: reduce_columns(): return lax.all_gather(piece, 'rep', axis=0, tiled=True).astype(f32)]
    all_to_all x4 -> x2, waiting for transfers between devices: 46.8 us -> 25.7 us  [the longest x1 25.7 us: body(): lax.all_to_all(fc1_weight, 'grp', split_axis=1, concat_axis=0, tiled=True)]
    all_gather x8 -> x2, blocking collectives: 42.3 us -> 63.1 us  [the longest x1 31.6 us: reduce_rows(): return lax.all_gather(piece, 'rep', axis=0, tiled=True).astype(f32)]
    all_to_all x0 -> x2, blocking collectives: none -> 18.9 us  [reduce_columns(): lax.all_to_all(piece, 'grp', split_axis=0, concat_axis=0, tiled=True)]
    pallas_call x0 -> x1, Pallas kernels: none -> 17.7 us  [attention(): pl.pallas_call(functools.partial(attention_kernel, block), grid=(pairs,),...]
  transfers between devices with their start and end apart: 16 -> 13, of which waited for: 13 -> 10; matrix products, arithmetic and copies ran while one was open for 14% -> 14% of each run, Pallas kernels for 0% -> 0%
where the time goes in v1:
time: 601 us; the launch traced here: 594 us
  waiting for transfers between devices  335 us (56%)
  blocking collectives  121 us (20%)
  matrix products  44.6 us (7%)
  local copies, waits for them, and re-layouts  31.7 us (5%)
  other arithmetic  20.2 us (3%)
  Pallas kernels  17.7 us (3%)
  between operations  14.9 us (2%)
  starting transfers between devices  9.53 us (2%)
    all_gather x2, waiting for transfers between devices, reduce_columns(): return lax.all_gather(piece, 'rep', axis=0, tiled=True).astype(f32)  90.2 us
    reduce_scatter x2, waiting for transfers between devices, reduce_columns(): piece = lax.psum_scatter(g, 'rep', scatter_dimension=0, tiled=True)  70.6 us
    reduce_scatter x2, waiting for transfers between devices, reduce_rows(): lax.psum_scatter(grad.astype(bf16), 'rep', scatter_dimension=0, tiled=True)  55.1 us
    all_gather x1, waiting for transfers between devices, reduce_rows(): return lax.all_gather(piece, 'rep', axis=0, tiled=True).astype(f32)  46.7 us
    psum x1, blocking collectives, body(): flat = lax.psum(flat, ('grp', 'rep'))  39.1 us
    reduce_scatter x1, waiting for transfers between devices, body(): lax.psum_scatter(branch.astype(bf16), 'grp', scatter_dimension=0, tiled=T...  33.2 us
    all_gather x1, blocking collectives, reduce_rows(): return lax.all_gather(piece, 'rep', axis=0, tiled=True).astype(f32)  31.6 us
    all_gather x1, blocking collectives, body(): lax.all_gather(jnp.concatenate(vectors), 'grp', axis=0, tiled=False)  31.4 us
  transfers between devices with their start and end apart: 13, of which 10 were waited for; matrix products, arithmetic and copies ran while one was open for 14% of the time, Pallas kernels for 0%

profile of v1, /device:TPU:0, one launch (start us, length us, event | category | flops | bytes accessed | tf_op | source)
XLA Modules:
  0.0 594.5 jit_solution(11829848551077639108)
XLA Ops:
  14.0 4.5 all-to-all-start
  19.9 31.4 %all-gather.3 = bf16[4,1,2304]{2,1,0:T(2,128)(2,1)S(1)} all-gather(bf16[1,1,2304]{2,1,0:T(2,128)(2,1)S(1)} %reshape.213), channel_id=3, replica_groups=mesh['grp'=4,'rep'=8] {'grp'}, dimensions={0}, use_global_device_ids=true | all-gather | bytes 23040 | tf_op jit(solution)/shard_map/all_gather | solution.py:197
  58.8 10.9 %all-gather.18.cloned.1.call-done = bf16[1,1024,1024]{2,1,0:T(8,128)(2,1)} async-done(((bf16[1,256,1024]{2,1,0:T(8,128)(2,1)}), bf16[1,1024,1024]{2,1,0:T(8,128)(2,1)}) %all-gather.18.cloned.1.call-update) | async-done | bytes 2097168 | tf_op jit(solution)/shard_map/all_gather | solution.py:195
  74.5 17.7 %shard_map.281 = (bf16[1024,256]{1,0:T(8,128)(2,1)S(1)}, bf16[1024,256]{1,0:T(8,128)(2,1)S(1)}, bf16[1024,256]{1,0:T(8,128)(2,1)S(1)}, bf16[1024,256]{1,0:T(8,128)(2,1)S(1)}, f32[8,256]{1,0:T(8,128)S(1)}) custom-call(f32[1024,768]{1,0:T(8,128)S(1)} %convolution_add_fusion.q_ref.k_ref.v_ref, f32[1024,768]{1,0:T(8,128)S(1)} %convolution_add_fusion.q_ref.k_ref.v_ref, ...), custom_call_target="tpu_custom_call" | custom-call | flops 2684354560 | bytes 6291456 | tf_op jit(solution)/shard_map/pallas_call | solution.py:143
  96.1 4.1 copy.59
  100.2 4.6 all-to-all-start.1
  104.9 25.7 %all-to-all-done.1 = bf16[256,4,1024]{0,2,1:T(8,128)(2,1)} async-done(((bf16[256,4,1024]{0,2,1:T(8,128)(2,1)}), bf16[256,4,1024]{0,2,1:T(8,128)(2,1)}, u32[]{:S(2)}, u32[]{:S(2)}) %all-to-all-start.1) | async-done | bytes 2097184 | tf_op jit(solution)/shard_map/all_to_all | solution.py:206
  130.5 4.1 copy.60
  134.7 6.6 %multiply_convert_fusion = (bf16[1024,1024]{1,0:T(8,128)(2,1)S(1)}, f32[1024,1024]{1,0:T(8,128)}) fusion(f32[1024]{0:T(1024)S(1)} %convert_element_type.149, bf16[1024,1024]{1,0:T(8,128)(2,1)} %bitcast.176, bf16[1,1024,1024]{2,1,0:T(8,128)(2,1)} %all-gather.16.cloned.1.call-done, f32[1024]{0:T(1024)S(1)} %bitcast.203, f32[1024]{0:T(1024)S(1)} %bitcast.198, ...), kind=kOutput, calls=%fused_computation.24 | convolution fusion | flops 2160066560 | bytes 10506240 | tf_op jit(solution)/shard_map/dot_general | solution.py:240
  146.5 6.4 %fusion.61 = (f32[1024]{0:T(1024)S(1)}, bf16[1024,1024]{1,0:T(8,128)(2,1)S(1)}) fusion(f32[1024,1024]{1,0:T(8,128)} %get-tuple-element.45, f32[1024]{0:T(1024)S(1)} %convert_element_type.149, bf16[1024,1024]{1,0:T(8,128)(2,1)S(1)} %copy-done, bf16[1,1024,1024]{2,1,0:T(8,128)(2,1)} %all-gather.18.cloned.1.call-done), kind=kOutput, calls=%fused_computation.96 | convolution fusion | flops 2160065536 | bytes 10493952 | tf_op jit(solution)/shard_map/dot_general | solution.py:46
  164.5 5.0 fusion.58
  175.7 9.5 %all_to_all.44 = bf16[4,32,768]{2,1,0:T(8,128)(2,1)} all-to-all(bf16[4,32,768]{2,1,0:T(8,128)(2,1)} %bitcast.187), channel_id=1, replica_groups=mesh['grp'=4,'rep'=8] {'grp'}, dimensions={0} | all-to-all | bytes 393216 | tf_op jit(solution)/shard_map/all_to_all | solution.py:220
  189.0 42.6 %reduce-scatter.17.cloned.1.call-done = bf16[128,1024]{1,0:T(8,128)(2,1)} async-done(((bf16[1024,1024]{1,0:T(8,128)(2,1)}), bf16[128,1024]{1,0:T(8,128)(2,1)}) %reduce-scatter.17.cloned.1.call-update) | async-done | bytes 262160 | tf_op jit(solution)/shard_map/reduce_scatter | solution.py:211
  231.7 70.6 %reduce-scatter.15.cloned.1.call-done = bf16[128,1024]{1,0:T(8,128)(2,1)} async-done(((bf16[1024,1024]{1,0:T(8,128)(2,1)}), bf16[128,1024]{1,0:T(8,128)(2,1)}) %reduce-scatter.15.cloned.1.call-update) | async-done | bytes 262160 | tf_op jit(solution)/shard_map/reduce_scatter | solution.py:218
  302.3 9.4 %all_to_all.45 = bf16[4,32,1024]{2,1,0:T(8,128)(2,1)S(1)} all-to-all(bf16[4,32,1024]{2,1,0:T(8,128)(2,1)} %bitcast.186), channel_id=1, replica_groups=mesh['grp'=4,'rep'=8] {'grp'}, dimensions={0} | all-to-all | bytes 524288 | tf_op jit(solution)/shard_map/all_to_all | solution.py:220
  313.9 39.1 %psum.7 = f32[4,3072]{1,0:T(4,128)S(1)} all-reduce(f32[4,3072]{1,0:T(4,128)S(1)} %constant_dynamic-update-slice_fusion.3), channel_id=1, replica_groups=mesh['grp'=4,'rep'=8] {'grp','rep'}, use_global_device_ids=true, to_apply=%region_14.0 | all-reduce | flops 12288 | bytes 98304 | tf_op jit(solution)/shard_map/psum | solution.py:285
  355.0 12.5 %reduce-scatter.13.cloned.1.call-done = bf16[32,1024]{1,0:T(8,128)(2,1)} async-done(((bf16[256,1024]{1,0:T(8,128)(2,1)}), bf16[32,1024]{1,0:T(8,128)(2,1)}) %reduce-scatter.13.cloned.1.call-update) | async-done | bytes 65552 | tf_op jit(solution)/shard_map/reduce_scatter | solution.py:211
  367.5 31.6 %all_gather.29 = bf16[256,1024]{1,0:T(8,128)(2,1)S(1)} all-gather(bf16[32,1024]{1,0:T(8,128)(2,1)} %reduce-scatter.13.cloned.1.call-done), channel_id=1, replica_groups=mesh['grp'=4,'rep'=8] {'rep'}, dimensions={0}, use_global_device_ids=true | all-gather | bytes 589824 | tf_op jit(solution)/shard_map/all_gather | solution.py:212
  402.6 33.2 %reduce-scatter.7.cloned.1.call-done = bf16[256,1024]{1,0:T(8,128)(2,1)} async-done(((bf16[1024,1024]{1,0:T(8,128)(2,1)}), bf16[256,1024]{1,0:T(8,128)(2,1)}) %reduce-scatter.7.cloned.1.call-update) | async-done | bytes 524304 | tf_op jit(solution)/shard_map/reduce_scatter | solution.py:258
  438.5 43.8 %all-gather.10.cloned.1.call-done = bf16[256,3072]{1,0:T(8,128)(2,1)} async-done(((bf16[32,3072]{1,0:T(8,128)(2,1)}), bf16[256,3072]{1,0:T(8,128)(2,1)}) %all-gather.10.cloned.1.call-update) | async-done | bytes 1572880 | tf_op jit(solution)/shard_map/all_gather | solution.py:223
  485.7 46.7 %all-gather.14.cloned.1.call-done = bf16[1024,1024]{1,0:T(8,128)(2,1)} async-done(((bf16[128,1024]{1,0:T(8,128)(2,1)}), bf16[1024,1024]{1,0:T(8,128)(2,1)}) %all-gather.14.cloned.1.call-update) | async-done | bytes 2097168 | tf_op jit(solution)/shard_map/all_gather | solution.py:212
  532.3 4.1 convert_element_type.168
  536.4 46.4 %all-gather.12.cloned.1.call-done = bf16[256,4096]{1,0:T(8,128)(2,1)} async-done(((bf16[32,4096]{1,0:T(8,128)(2,1)}), bf16[256,4096]{1,0:T(8,128)(2,1)}) %all-gather.12.cloned.1.call-update) | async-done | bytes 2097168 | tf_op jit(solution)/shard_map/all_gather | solution.py:223
  582.9 4.1 convert_element_type.166
  (168 shorter events, 64.9 us)
Async XLA Ops:
  7.2 139.3 %copy-start = (bf16[1024,1024]{1,0:T(8,128)(2,1)S(1)}, bf16[1024,1024]{1,0:T(8,128)(2,1)}, u32[]{:S(2)}) copy-start(bf16[1024,1024]{1,0:T(8,128)(2,1)} %param.30) | copy-start | bytes 6291460
  7.2 48.7 %all-gather.16.cloned.1.call-start = ((), (), s32[]{:S(2)}) async-start(), calls=%async_computation.19 | async-start | bytes 2621440 | tf_op jit(solution)/shard_map/all_gather | solution.py:194
  7.9 61.8 %all-gather.18.cloned.1.call-start = ((), (), s32[]{:S(2)}) async-start(), calls=%async_computation.20 | async-start | bytes 2621440 | tf_op jit(solution)/shard_map/all_gather | solution.py:195
  13.9 5.5 copy-start.19
  13.9 5.7 copy-start.24
  13.9 5.9 copy-start.25
  14.0 37.5 %copy-start.4 = (s32[1,1024]{1,0:T(1,128)S(1)}, s32[1,1024]{1,0:T(1,128)}, u32[]{:S(2)}) copy-start(s32[1,1024]{1,0:T(1,128)} %drow_ref.1) | copy-start | bytes 12292
  14.0 37.7 %all-to-all-start = ((bf16[256,3,4,256]{0,3,1,2:T(8,128)(2,1)}), bf16[256,3,4,256]{0,3,1,2:T(8,128)(2,1)}, u32[]{:S(2)}, u32[]{:S(2)}) async-start(bf16[256,3,4,256]{0,3,1,2:T(8,128)(2,1)} %copy.56), calls=%async_computation | async-start | bytes 3145728 | tf_op jit(solution)/shard_map/all_to_all | solution.py:203
  18.5 157.3 %reduce-scatter.11.cloned.1.call-start = ((), (), s32[]{:S(2)}) async-start(), calls=%async_computation.12 | async-start | bytes 1769472 | tf_op jit(solution)/shard_map/reduce_scatter | solution.py:218
  55.9 13.8 %copy-start.14 = (bf16[256,1024]{1,0:T(8,128)(2,1)S(1)}, bf16[256,1024]{1,0:T(8,128)(2,1)}, u32[]{:S(2)}) copy-start(bf16[256,1024]{1,0:T(8,128)(2,1)} %param.26) | copy-start | bytes 1572868
  100.2 30.4 %all-to-all-start.1 = ((bf16[256,4,1024]{0,2,1:T(8,128)(2,1)}), bf16[256,4,1024]{0,2,1:T(8,128)(2,1)}, u32[]{:S(2)}, u32[]{:S(2)}) async-start(bf16[256,4,1024]{0,2,1:T(8,128)(2,1)} %bitcast.172), calls=%async_computation.1 | async-start | bytes 4194304 | tf_op jit(solution)/shard_map/all_to_all | solution.py:206
  104.8 126.9 %reduce-scatter.17.cloned.1.call-start = ((), (), s32[]{:S(2)}) async-start(), calls=%async_computation.17 | async-start | bytes 2359296 | tf_op jit(solution)/shard_map/reduce_scatter | solution.py:211
  134.7 7.9 %copy-start.11 = (bf16[1,1024,1024]{2,1,0:T(8,128)(2,1)S(1)}, bf16[1,1024,1024]{2,1,0:T(8,128)(2,1)}, u32[]{:S(2)}) copy-start(bf16[1,1024,1024]{2,1,0:T(8,128)(2,1)} %all-gather.18.cloned.1.call-done) | copy-start | bytes 6291460
  146.4 155.9 %reduce-scatter.15.cloned.1.call-start = ((), (), s32[]{:S(2)}) async-start(), calls=%async_computation.15 | async-start | bytes 2359296 | tf_op jit(solution)/shard_map/reduce_scatter | solution.py:218
  146.4 6.5 %copy-start.8 = (bf16[1,1024,1024]{2,1,0:T(8,128)(2,1)S(1)}, bf16[1,1024,1024]{2,1,0:T(8,128)(2,1)}, u32[]{:S(2)}) copy-start(bf16[1,1024,1024]{2,1,0:T(8,128)(2,1)} %all-gather.16.cloned.1.call-done) | copy-start | bytes 6291460
  157.3 210.2 %reduce-scatter.13.cloned.1.call-start = ((), (), s32[]{:S(2)}) async-start(), calls=%async_computation.14 | async-start | bytes 589824 | tf_op jit(solution)/shard_map/reduce_scatter | solution.py:211
  160.5 240.6 %reduce-scatter.9.cloned.1.call-start = ((), (), s32[]{:S(2)}) async-start(), calls=%async_computation.11 | async-start | bytes 2621440 | tf_op jit(solution)/shard_map/reduce_scatter | solution.py:262
  169.5 266.3 %reduce-scatter.7.cloned.1.call-start = ((), (), s32[]{:S(2)}) async-start(), calls=%async_computation.10 | async-start | bytes 2621440 | tf_op jit(solution)/shard_map/reduce_scatter | solution.py:258
  175.7 137.1 %copy-start.10 = (bf16[1,256,1024]{2,1,0:T(8,128)(2,1)S(1)}, bf16[1,256,1024]{2,1,0:T(8,128)(2,1)}, u32[]{:S(2)}) copy-start(bf16[1,256,1024]{2,1,0:T(8,128)(2,1)} %param.32) | copy-start | bytes 1572868
  175.7 306.6 %all-gather.10.cloned.1.call-start = ((), (), s32[]{:S(2)}) async-start(), calls=%async_computation.13 | async-start | bytes 1769472 | tf_op jit(solution)/shard_map/all_gather | solution.py:223
  185.3 127.6 %copy-start.5 = (bf16[1,256,1024]{2,1,0:T(8,128)(2,1)S(1)}, bf16[1,256,1024]{2,1,0:T(8,128)(2,1)}, u32[]{:S(2)}) copy-start(bf16[1,256,1024]{2,1,0:T(8,128)(2,1)} %param.18) | copy-start | bytes 1572868
  189.0 343.4 %all-gather.14.cloned.1.call-start = ((), (), s32[]{:S(2)}) async-start(), calls=%async_computation.18 | async-start | bytes 2359296 | tf_op jit(solution)/shard_map/all_gather | solution.py:212
  231.6 351.2 %all-gather.12.cloned.1.call-start = ((), (), s32[]{:S(2)}) async-start(), calls=%async_computation.16 | async-start | bytes 2359296 | tf_op jit(solution)/shard_map/all_gather | solution.py:223
  354.3 232.6 %copy-start.17 = (f32[1,256]{1,0:T(1,128)}, f32[1,256]{1,0:T(1,128)S(1)}, u32[]{:S(2)}) copy-start(f32[1,256]{1,0:T(1,128)S(1)} %get-tuple-element.35) | copy-start | bytes 3076
  (18 other events, 60.6 us)
Sparse Core Ops, SparseCore 0:
  9.6 36.3 all-gather.15
  47.6 22.0 all-gather.17
  96.2 64.9 reduce-scatter.10
  165.0 66.6 reduce-scatter.16
  235.4 66.8 reduce-scatter.14
  306.4 61.0 reduce-scatter.12
  370.6 30.4 reduce-scatter.8
  404.4 31.4 reduce-scatter.6
  438.0 44.1 all-gather.9
  484.2 48.0 all-gather.13
  535.1 47.7 all-gather.11
